TPU v7x, 256 devices: a whole 4x4x8 slice. The times are simulated.
256 devices in a mesh: region: 32 (over y, x, z_lo), wshard: 8 (over z_hi, core).
Axes of the slice: x: 4, y: 4, z: 8 (z_hi: 4, z_lo: 2; z = z_hi * 2 + z_lo), core: 2. Of those that a mesh axis runs over, the one named last changes fastest.
Arguments:
- queries: bfloat16 [16384, 1024], P('region', 'wshard'), may hold values from -9 to 9
- mold: bfloat16 [65536, 1024], P('region', 'wshard'), may hold values from -9 to 9
- q_weight: bfloat16 [1024, 1024], P(None, 'wshard'), as said below
- k_weight: bfloat16 [1024, 256], replicated, as said below
- v_weight: bfloat16 [1024, 256], replicated, as said below
- o_weight: bfloat16 [1024, 1024], P('wshard'), may hold values from -0.75 to 0.75
- block_lists: int32 [128, 16], P('region'), may hold values from 0 to 511, as said below
- live_counts: int32 [32], P('region'), may hold values from 1 to 4
Outputs:
- mixed: bfloat16 [16384, 1024], P('region', 'wshard')
Inputs may be any that keep to these rules, and one draw needn't show every extreme that they name: `block_lists`: an entry of row b names a mold block of the query block's region r = b // 4 or of region r - 1 or r + 1; entries of one row may repeat. `q_weight`: entries lie within 6 / sqrt(1024) of zero. `k_weight`: entries lie within 6 / sqrt(1024) of zero. `v_weight`: entries lie within 6 / sqrt(1024) of zero.
All inputs are finite; a program needn't handle non-finite values.
Results may differ from a plain program's by a relative error of at most 0.022.
Values may be sent and summed in bfloat16 or wider, within the bound.
A program may use at most 64 MiB of HBM per device.

v0:
```python
import jax
import jax.numpy as jnp
from jax import lax
from jax.sharding import PartitionSpec as P

QUERY_HEADS = 16
KEY_VALUE_HEADS = 4
HEAD_SIZE = 64
BLOCK_TOKENS = 128


def padded(block, sides, width):
    for axis, dim in sides:
        count = lax.axis_size(axis)
        forward = [(i, i + 1) for i in range(count - 1)]
        backward = [(target, source) for source, target in forward]
        low = lax.ppermute(
            lax.slice_in_dim(block, block.shape[dim] - width, None, axis=dim), axis, forward
        )
        high = lax.ppermute(lax.slice_in_dim(block, 0, width, axis=dim), axis, backward)
        block = jnp.concatenate([low, block, high], axis=dim)
    return block


def attend_blocks(query_blocks, key_blocks, value_blocks, lists):
    count_q, rows, kv_heads, query_group, width = query_blocks.shape
    listed = lists.shape[1]
    scores = jnp.einsum(
        "bqhge,blshe->bhgqls", query_blocks, key_blocks, preferred_element_type=jnp.float32
    ) * width ** (-0.5)
    same_block = lists[:, :, None] == lists[:, None, :]
    earlier = jnp.tril(jnp.ones((listed, listed), dtype=bool), -1)
    repeated_heads = jnp.any(same_block & earlier[None], axis=2)
    scores = jnp.where(repeated_heads[:, None, None, None, :, None], -1e30, scores)
    scores = scores.reshape(count_q, kv_heads, query_group, rows, listed * rows)
    top = jnp.max(scores, axis=-1, keepdims=True)
    expo = jnp.exp(scores - top)
    probs = (expo / jnp.sum(expo, axis=-1, keepdims=True)).astype(jnp.bfloat16)
    value_rows = value_blocks.reshape(count_q, listed * rows, kv_heads, width)
    mixed_heads = jnp.einsum(
        "bhgqk,bkhe->bqhge", probs, value_rows, preferred_element_type=jnp.float32
    )
    return mixed_heads.reshape(count_q, rows, kv_heads * query_group * width).astype(jnp.bfloat16)


def shards(queries, mold, q_weight, k_weight, v_weight, o_weight, block_lists, live_counts):
    shard_index = lax.axis_index("wshard")
    heads_here = q_weight.shape[1] // HEAD_SIZE
    query_group = QUERY_HEADS // KEY_VALUE_HEADS
    kv_heads_here = max(heads_here // query_group, 1)
    group_here = heads_here // kv_heads_here
    kv_start = shard_index * heads_here // query_group
    key_columns = lax.dynamic_slice_in_dim(
        k_weight, kv_start * HEAD_SIZE, kv_heads_here * HEAD_SIZE, 1
    )
    value_columns = lax.dynamic_slice_in_dim(
        v_weight, kv_start * HEAD_SIZE, kv_heads_here * HEAD_SIZE, 1
    )
    pair_weight = jnp.concatenate([key_columns, value_columns], axis=1)
    query_rows = queries.shape[0]
    mold_rows = mold.shape[0]
    rows_w = q_weight
    q_local = jnp.dot(
        lax.all_gather(queries, "wshard", axis=1, tiled=True),
        rows_w,
        preferred_element_type=jnp.float32,
    ).astype(jnp.bfloat16)
    rows_w = pair_weight
    kv_pairs = jnp.dot(
        lax.all_gather(mold, "wshard", axis=1, tiled=True),
        rows_w,
        preferred_element_type=jnp.float32,
    ).astype(jnp.bfloat16)
    region_index = lax.axis_index("region")
    blocks_here = mold_rows // BLOCK_TOKENS
    key_pool = padded(kv_pairs, (("region", 0),), mold_rows)
    local_ids = block_lists - (region_index - 1) * blocks_here
    key_pool = key_pool.reshape(-1, BLOCK_TOKENS, 2, kv_heads_here, HEAD_SIZE)
    fetched = jnp.take(key_pool, local_ids, axis=0)
    key_blocks = fetched[:, :, :, 0]
    value_blocks = fetched[:, :, :, 1]
    query_blocks = q_local.reshape(
        query_rows // BLOCK_TOKENS, BLOCK_TOKENS, kv_heads_here, group_here, HEAD_SIZE
    )
    attn = attend_blocks(query_blocks, key_blocks, value_blocks, block_lists)
    live_rows = jnp.arange(query_rows // BLOCK_TOKENS, dtype=jnp.int32) < live_counts[0]
    attn = jnp.where(live_rows[:, None, None], attn, jnp.zeros_like(attn))
    flat_attn = attn.reshape(query_rows, heads_here * HEAD_SIZE)
    head_terms = jnp.dot(flat_attn, o_weight, preferred_element_type=jnp.float32)
    return lax.psum_scatter(
        head_terms.astype(jnp.bfloat16), "wshard", scatter_dimension=1, tiled=True
    )


def solution(mesh):
    return jax.shard_map(
        shards,
        mesh=mesh,
        in_specs=(
            P("region", "wshard"),
            P("region", "wshard"),
            P(None, "wshard"),
            P(),
            P(),
            P("wshard", None),
            P("region", None),
            P("region"),
        ),
        out_specs=P("region", "wshard"),
        check_vma=False,
    )
```

profile of v0, /device:TPU:1, one launch (start us, length us, event | category | flops | bytes accessed | tf_op | source)
XLA Modules:
  0.0 169.7 jit_solution(13676864286253016026)
XLA Ops:
  6.5 0.7 all-gather.3.cloned.1.call-update
  7.3 0.7 all-gather.5.cloned.1.call-update
  8.7 0.7 compare_and_fusion
  9.6 1.0 and_reduce_fusion
  10.6 1.2 constant_dynamic-slice_fusion
  11.8 59.2 %all-gather.3.cloned.1.call-done = bf16[2048,1024]{1,0:T(8,128)(2,1)} async-done(((bf16[2048,128]{1,0:T(8,128)(2,1)}), bf16[2048,1024]{1,0:T(8,128)(2,1)}) %all-gather.3.cloned.1.call-update) | async-done | bytes 4194320 | tf_op jit(solution)/shard_map/all_gather | solution.py:70
  71.0 3.9 %fusion.2 = bf16[2048,128]{0,1:T(8,128)(2,1)S(1)} fusion(bf16[2048,1024]{1,0:T(8,128)(2,1)} %all-gather.3.cloned.1.call-done, bf16[1024,64]{1,0:T(8,128)(2,1)S(1)} %get-tuple-element.9, bf16[1024,64]{1,0:T(8,128)(2,1)S(1)} %get-tuple-element.10), kind=kOutput, calls=%fused_computation.7 | convolution fusion | flops 537657344 | bytes 4980736 | tf_op jit(solution)/shard_map/dot_general | solution.py:69
  75.0 1.3 collective-permute-start.1
  76.3 4.0 %collective-permute-start = (bf16[2048,128]{0,1:T(8,128)(2,1)S(1)}, bf16[2048,128]{0,1:T(8,128)(2,1)S(1)}, u32[]{:S(2)}, u32[]{:S(2)}) collective-permute-start(bf16[2048,128]{0,1:T(8,128)(2,1)S(1)} %fusion.2), channel_id=1, source_target_pairs={{0,8},{8,16},{16,24},{24,32},{32,40},{40,48},{48,56},{56,64},{64,7... | collective-permute-start | bytes 1572872 | tf_op jit(solution)/shard_map/ppermute | solution.py:17
  80.4 25.2 %all-gather.5.cloned.1.call-done = bf16[512,1024]{1,0:T(8,128)(2,1)} async-done(((bf16[512,128]{1,0:T(8,128)(2,1)}), bf16[512,1024]{1,0:T(8,128)(2,1)}) %all-gather.5.cloned.1.call-update) | async-done | bytes 1048592 | tf_op jit(solution)/shard_map/all_gather | solution.py:64
  105.6 1.7 convolution_convert_fusion.2
  107.2 0.9 reshape.106
  109.0 2.2 %gather_fusion = bf16[64,128,2,64]{1,3,2,0:T(8,128)(2,1)} fusion(bf16[48,128,2,64]{1,3,2,0:T(8,128)(2,1)S(1)} %copy.27, s32[1024]{0:T(1024)S(1)} %pad_clamp_fusion), kind=kCustom, calls=%fused_computation | custom fusion | bytes 4194560 | tf_op jit(solution)/shard_map/jit(_take)/gather | solution.py:79
  111.1 1.8 %copy.28 = bf16[64,128,2,64]{1,3,0,2:T(8,128)(2,1)S(1)} copy(bf16[64,128,2,64]{1,3,2,0:T(8,128)(2,1)} %gather_fusion) | data formatting | bytes 4194304 | tf_op jit(solution)/shard_map/jit(_take)/gather | solution.py:79
  113.3 0.7 copy.29
  114.0 1.3 reshape.104
  115.2 2.7 %fusion.15 = (f32[4,2,128]{2,1,0:T(2,128)S(1)}, f32[4,1,2,128,16,128]{3,5,2,4,0,1:T(8,128)S(1)}) fusion(bf16[4,128,2,64,1]{3,2,1,0,4:T(2,128)(2,1)} %bitcast.58, bf16[4,16,128,2,1,64]{2,5,1,0,4,3:T(8,128)(2,1)S(1)} %broadcast_select_fusion, pred[4,16]{1,0:T(4,128)(4,1)S(1)} %and_reduce_fusion), kind=kOutput, calls=%fused_computation.36 | convolution fusion | flops 274725888 | bytes 9572864 | tf_op jit(solution)/shard_map/bqhge,blshe->bhgqls/dot_general | solution.py:28
  118.0 1.1 copy.32
  119.1 1.1 exponential_reduce_fusion
  120.3 1.5 fusion.4
  122.0 0.5 convolution_convert_fusion.1
  122.4 1.3 copy.43
  123.8 37.8 %reduce-scatter.4.cloned.1.call-done = bf16[128,512]{1,0:T(8,128)(2,1)} async-done(((bf16[1024,512]{1,0:T(8,128)(2,1)}), bf16[128,512]{1,0:T(8,128)(2,1)}) %reduce-scatter.4.cloned.1.call-update) | async-done | bytes 131088
  161.5 1.7 copy.44
  (24 shorter events, 1.8 us)
Async XLA Ops:
  6.5 115.4 %copy-start = (bf16[128,1024]{1,0:T(8,128)(2,1)S(1)}, bf16[128,1024]{1,0:T(8,128)(2,1)}, u32[]{:S(2)}) copy-start(bf16[128,1024]{1,0:T(8,128)(2,1)} %param.13) | copy-start | bytes 786436
  6.5 99.0 %copy-start.2 = (bf16[1024,128]{1,0:T(8,128)(2,1)S(1)}, bf16[1024,128]{1,0:T(8,128)(2,1)}, u32[]{:S(2)}) copy-start(bf16[1024,128]{1,0:T(8,128)(2,1)} %param.10) | copy-start | bytes 786436
  6.5 64.5 %all-gather.3.cloned.1.call-start = ((), (), s32[]{:S(2)}) async-start(), calls=%async_computation.1 | async-start | bytes 4718592 | tf_op jit(solution)/shard_map/all_gather | solution.py:70
  7.3 98.3 %all-gather.5.cloned.1.call-start = ((), (), s32[]{:S(2)}) async-start(), calls=%async_computation.2 | async-start | bytes 1179648 | tf_op jit(solution)/shard_map/all_gather | solution.py:64
  8.0 153.5 %reduce-scatter.4.cloned.1.call-start = ((), (), s32[]{:S(2)}) async-start(), calls=%async_computation.3 | async-start | bytes 1179648
  75.0 33.1 %collective-permute-start.1 = (bf16[2048,128]{0,1:T(8,128)(2,1)S(1)}, bf16[2048,128]{0,1:T(8,128)(2,1)S(1)}, u32[]{:S(2)}, u32[]{:S(2)}) collective-permute-start(bf16[2048,128]{0,1:T(8,128)(2,1)S(1)} %fusion.2), channel_id=1, source_target_pairs={{8,0},{16,8},{24,16},{32,24},{40,32},{48,40},{56,48},{64,56},{72,6... | collective-permute-start | bytes 1572872 | tf_op jit(solution)/shard_map/ppermute | solution.py:20
  76.3 31.8 %collective-permute-start = (bf16[2048,128]{0,1:T(8,128)(2,1)S(1)}, bf16[2048,128]{0,1:T(8,128)(2,1)S(1)}, u32[]{:S(2)}, u32[]{:S(2)}) collective-permute-start(bf16[2048,128]{0,1:T(8,128)(2,1)S(1)} %fusion.2), channel_id=1, source_target_pairs={{0,8},{8,16},{16,24},{24,32},{32,40},{40,48},{48,56},{56,64},{64,7... | collective-permute-start | bytes 1572872 | tf_op jit(solution)/shard_map/ppermute | solution.py:17
  119.1 1.2 copy-start.1
Sparse Core Ops, SparseCore 0:
  9.2 61.8 all-gather.2
  72.9 32.6 all-gather.4
  123.9 37.5 reduce-scatter.3
where the time goes:
time: 171 us; the launch traced here: 170 us
  waiting for transfers between devices  124 us (73%)
  between operations  13.9 us (8%)
  local copies, waits for them, and re-layouts  13.3 us (8%)
  matrix products  10.3 us (6%)
  starting transfers between devices  5.39 us (3%)
  other arithmetic  3.23 us (2%)
    all_gather x1, waiting for transfers between devices, shards(): lax.all_gather(mold, 'wshard', axis=1, tiled=True)  59.2 us
    unnamed x4, waiting for transfers between devices  39.2 us
    all_gather x1, waiting for transfers between devices, shards(): lax.all_gather(queries, 'wshard', axis=1, tiled=True)  25.2 us
    ppermute x1, starting transfers between devices, padded(): lax.ppermute(lax.slice_in_dim(block, block.shape[dim] - width, None, axis...  4.02 us
    gather x2, local copies, waits for them, and re-layouts, shards(): fetched = jnp.take(key_pool, local_ids, axis=0)  3.93 us
    dot_general x1, matrix products, shards(): jnp.dot(lax.all_gather(mold, 'wshard', axis=1, tiled=True), rows_w, prefe...  3.9 us
    unnamed x9, local copies, waits for them, and re-layouts  3.47 us
  transfers between devices with their start and end apart: 5, of which 3 were waited for; matrix products, arithmetic and copies ran while one was open for 6% of the time, Pallas kernels for 0%

commit v1 on v0

v1 whole, which is shorter than its diff:
```python
import functools

import jax
import jax.numpy as jnp
from jax import lax
from jax.experimental import pallas as pl
from jax.experimental.pallas import tpu as pltpu
from jax.sharding import PartitionSpec as P

HEAD = 64
KV_HEADS = 4
BLOCK = 128
MESH = pl.DeviceIdType.MESH
CHUNKS = 2
F32, BF16 = jnp.float32, jnp.bfloat16


def kernel(
    chips,
    regions,
    queries,
    mold,
    q_weight,
    k_weight,
    v_weight,
    o_weight,
    lists,
    live,
    out,
    q_own,
    q_all,
    qw,
    kw,
    vw,
    wkv,
    ow,
    mold_own,
    mold_z,
    mold_c,
    kv_send,
    pool,
    kv_list,
    q_ext,
    scores,
    bias,
    attn,
    part,
    part_own,
    got,
    sem_local,
    mz_s,
    mz_r,
    mc_s,
    mc_r,
    kz_s,
    kz_r,
    kc_s,
    kc_r,
    ki_s,
    ki_r,
    kx_s,
    kx_r,
    qz_s,
    qz_r,
    qc_s,
    qc_r,
    ow_s,
    ow_r,
    ac_s,
    ac_r,
    oz_s,
    oz_r,
):
    region = lax.axis_index("region")
    shard = lax.axis_index("wshard")
    chip = shard // 2
    core = lax.rem(shard, 2)
    other = 1 - core
    odd = lax.rem(region, 2)
    qblocks, listed = lists.shape
    pool_blocks = pool.shape[0] // 3
    chip_blocks = pool_blocks // chips
    chip_rows = chip_blocks * BLOCK
    rows_j = chip_rows // CHUNKS
    half = rows_j // 2
    piece = half // BLOCK
    far = range(1, chips)
    near = range(chips)

    def ahead(d):
        return lax.rem(chip + d, chips)

    def behind(d):
        return lax.rem(chip + chips - d, chips)

    def z_peer(d):
        return (region, ahead(d) * 2 + core)

    core_peer = (region, chip * 2 + other)
    sibling = (region + 1 - 2 * odd, shard)
    x_to = (lax.rem(region + regions + 2 - 4 * odd, regions), shard)
    x_from = (lax.rem(region + regions - 2 + 4 * odd, regions), shard)

    def remote(src, dst, send, recv, peer):
        return pltpu.make_async_remote_copy(
            src_ref=src, dst_ref=dst, send_sem=send, recv_sem=recv, device_id=peer, device_id_type=MESH
        )

    local = [
        pltpu.make_async_copy(k_weight, kw, sem_local.at[0]),
        pltpu.make_async_copy(v_weight, vw, sem_local.at[1]),
        pltpu.make_async_copy(q_weight, qw, sem_local.at[2]),
        pltpu.make_async_copy(o_weight, ow.at[core], sem_local.at[3]),
        pltpu.make_async_copy(queries, q_own, sem_local.at[4]),
        pltpu.make_async_copy(
            mold.at[pl.ds(pl.multiple_of(chip * chip_rows, BLOCK), chip_rows)], mold_own, sem_local.at[5]
        ),
    ]
    for copy in (local[5], local[0], local[1], local[4], local[2], local[3]):
        copy.start()

    barrier = pltpu.get_barrier_semaphore()
    partners = [z_peer(d) for d in far] + [core_peer, sibling, x_to, x_from]
    for peer in partners:
        pl.semaphore_signal(barrier, inc=1, device_id=peer, device_id_type=MESH)
    pl.semaphore_wait(barrier, len(partners))

    def mold_z_copy(j, d):
        row = pl.multiple_of(ahead(d) * chip_rows + j * rows_j, BLOCK)
        return remote(
            mold.at[pl.ds(row, rows_j)], mold_z.at[j, d - 1], mz_s.at[j, d - 1], mz_r.at[j, d - 1], z_peer(d)
        )

    for j in range(CHUNKS):
        for d in far:
            mold_z_copy(j, d).start()

    def mold_src(j, d, side):
        rows = pl.ds(pl.multiple_of(side * half, BLOCK), half)
        if d == 0:
            return mold_own.at[pl.ds(pl.multiple_of(j * rows_j + side * half, BLOCK), half)]
        return mold_z.at[j, d - 1, rows]

    def mold_c_copy(j, d):
        return remote(mold_src(j, d, other), mold_c.at[j, d], mc_s.at[j, d], mc_r.at[j, d], core_peer)

    local[5].wait()
    for j in range(CHUNKS):
        mold_c_copy(j, 0).start()

    local[0].wait()
    local[1].wait()
    for h in range(KV_HEADS):
        cols = slice(h * HEAD, (h + 1) * HEAD)
        wkv[:, h * 2 * HEAD : (h + 1) * 2 * HEAD] = jnp.concatenate([kw[:, cols], vw[:, cols]], axis=1)

    def mark(i, _):
        for l in range(listed):
            repeat = jnp.int32(0)
            for e in range(l):
                repeat = jnp.where(lists[i, e] == lists[i, l], jnp.int32(1), repeat)
            bias[i, l] = jnp.where(repeat == 1, F32(-1e30), F32(0.0))
        return 0

    lax.fori_loop(0, qblocks, mark, 0)

    local[3].wait()
    ow_copy = remote(ow.at[core], ow.at[core], ow_s, ow_r, core_peer)
    ow_copy.start()

    def at_piece(slot, j, d, side):
        return pl.ds(slot * pool_blocks + behind(d) * chip_blocks + (j * 2 + side) * piece, piece)

    def kv_z_copy(j, d):
        spot = at_piece(0, j, 0, core)
        return remote(kv_send.at[j, ahead(d)], pool.at[spot], kz_s.at[j, d - 1], kz_r.at[j, d - 1], z_peer(d))

    def kv_z_got(j, d):
        spot = at_piece(0, j, d, core)
        return remote(kv_send.at[j, 0], pool.at[spot], kz_s.at[j, d - 1], kz_r.at[j, d - 1], z_peer(d))

    def kv_core(slot, j, d):
        spot = at_piece(slot, j, d, core)
        return remote(pool.at[spot], pool.at[spot], kc_s.at[slot, j, d], kc_r.at[slot, j, d], core_peer)

    def kv_core_got(slot, j, d):
        spot = at_piece(slot, j, d, other)
        return remote(pool.at[spot], pool.at[spot], kc_s.at[slot, j, d], kc_r.at[slot, j, d], core_peer)

    def kv_sib(j, d):
        return remote(
            pool.at[at_piece(0, j, d, core)],
            pool.at[at_piece(1, j, d, core)],
            ki_s.at[j, d],
            ki_r.at[j, d],
            sibling,
        )

    def kv_x(j, d):
        return remote(
            pool.at[at_piece(1, j, d, core)],
            pool.at[at_piece(2, j, d, core)],
            kx_s.at[j, d],
            kx_r.at[j, d],
            x_to,
        )

    def q_z_copy(d):
        return remote(queries, q_all.at[shard], qz_s.at[d - 1], qz_r.at[d - 1], z_peer(d))

    def q_z_got(d):
        return remote(queries, q_all.at[behind(d) * 2 + core], qz_s.at[d - 1], qz_r.at[d - 1], z_peer(d))

    def q_core(d):
        if d == 0:
            return remote(queries, q_all.at[shard], qc_s.at[0], qc_r.at[0], core_peer)
        slot = behind(d) * 2 + core
        return remote(q_all.at[slot], q_all.at[slot], qc_s.at[d], qc_r.at[d], core_peer)

    def q_core_got(d):
        slot = behind(d) * 2 + other
        return remote(queries, q_all.at[slot], qc_s.at[d], qc_r.at[d], core_peer)

    q_core(0).start()

    for j in range(CHUNKS):
        for d in far:
            mold_z_copy(j, d).wait_recv()
            mold_c_copy(j, d).start()
        total = jnp.zeros((half, wkv.shape[1]), F32)
        for d in near:
            depth = 2 * BLOCK
            base = pl.multiple_of(behind(d) * depth, depth)
            mine = wkv[pl.ds(pl.multiple_of(base + core * BLOCK, BLOCK), BLOCK), :]
            total += jnp.dot(mold_src(j, d, core)[...], mine, preferred_element_type=F32)
            mold_c_copy(j, d).wait_recv()
            theirs = wkv[pl.ds(pl.multiple_of(base + other * BLOCK, BLOCK), BLOCK), :]
            total += jnp.dot(mold_c[j, d], theirs, preferred_element_type=F32)
        pairs = total.astype(BF16)
        for h in range(KV_HEADS):
            kv_send[j, h] = pairs[:, h * BLOCK : (h + 1) * BLOCK].reshape(piece, BLOCK, BLOCK)
        pool[at_piece(0, j, 0, core)] = kv_send[j, chip]
        for d in far:
            kv_z_copy(j, d).start()
        kv_sib(j, 0).start()
        kv_core(0, j, 0).start()

    for d in far:
        q_z_copy(d).start()

    for j in range(CHUNKS):
        for d in far:
            kv_z_got(j, d).wait_recv()
            kv_sib(j, d).start()
            kv_core(0, j, d).start()
    for j in range(CHUNKS):
        for d in near:
            kv_sib(j, d).wait_recv()
            kv_x(j, d).start()
            kv_core(1, j, d).start()
    for d in far:
        q_z_got(d).wait_recv()
        q_core(d).start()
    for j in range(CHUNKS):
        for d in near:
            kv_x(j, d).wait_recv()
            kv_core(2, j, d).start()

    local[4].wait()
    local[2].wait()
    rows_q = q_own.shape[0]

    def weight_rows(s):
        return qw[pl.ds(pl.multiple_of(s * BLOCK, BLOCK), BLOCK), :]

    q_sum = jnp.dot(q_own[...], weight_rows(shard), preferred_element_type=F32)
    q_core_got(0).wait_recv()
    q_sum += jnp.dot(q_all[chip * 2 + other], weight_rows(chip * 2 + other), preferred_element_type=F32)
    for d in far:
        s = behind(d) * 2 + core
        q_sum += jnp.dot(q_all[s], weight_rows(s), preferred_element_type=F32)
        q_core_got(d).wait_recv()
        s = behind(d) * 2 + other
        q_sum += jnp.dot(q_all[s], weight_rows(s), preferred_element_type=F32)
    q_scaled = q_sum.astype(BF16).astype(F32) * HEAD**-0.5
    lane = lax.broadcasted_iota(jnp.int32, (rows_q, 2 * HEAD), 1)
    first = jnp.where(lane < HEAD, q_scaled, 0.0).astype(BF16)
    second = jnp.where(lane < HEAD, pltpu.roll(q_scaled, HEAD, 1), 0.0).astype(BF16)
    for i in range(qblocks):
        rows = slice(i * BLOCK, (i + 1) * BLOCK)
        q_ext[i, :BLOCK] = first[rows]
        q_ext[i, BLOCK:] = second[rows]

    for slot in range(3):
        for j in range(CHUNKS):
            for d in near:
                kv_core_got(slot, j, d).wait_recv()
    ow_copy.wait_recv()

    low = lax.broadcasted_iota(jnp.int32, (BLOCK, 2 * HEAD), 1) < HEAD
    wide = 2 * BLOCK

    def attn_copy(i):
        return remote(attn.at[core, i], attn.at[core, i], ac_s.at[i], ac_r.at[i], core_peer)

    def attn_got(i):
        return remote(attn.at[other, i], attn.at[other, i], ac_s.at[i], ac_r.at[i], core_peer)

    def part_copy(i, d):
        return remote(part.at[i, d - 1], got.at[i, d - 1], oz_s.at[i, d - 1], oz_r.at[i, d - 1], z_peer(d))

    def attend(i):
        for l in range(listed):
            block = lists[i, l]
            home = block // pool_blocks
            slot = jnp.where(home == region, 0, jnp.where(home == sibling[0], 1, 2))
            kv_list[l * BLOCK : (l + 1) * BLOCK] = pool[slot * pool_blocks + lax.rem(block, pool_blocks)]
        q = q_ext[i]
        top = jnp.full((wide, BLOCK), -jnp.inf, F32)
        for p in range(listed // 2):
            keys = kv_list[p * wide : (p + 1) * wide]
            s = lax.dot_general(q, keys, (((1,), (1,)), ((), ())), preferred_element_type=F32)
            for e in range(2):
                se = s[:, e * BLOCK : (e + 1) * BLOCK] + bias[i, 2 * p + e]
                scores[:, p * wide + e * BLOCK : p * wide + (e + 1) * BLOCK] = se
                top = jnp.maximum(top, se)
        top = jnp.max(top, axis=1, keepdims=True)
        total = jnp.zeros((wide, BLOCK), F32)
        mixed = jnp.zeros((wide, BLOCK), F32)
        for p in range(listed // 2):
            e = jnp.exp(scores[:, p * wide : (p + 1) * wide] - top)
            total += e[:, :BLOCK] + e[:, BLOCK:]
            mixed += jnp.dot(e.astype(BF16), kv_list[p * wide : (p + 1) * wide], preferred_element_type=F32)
        mixed = mixed / jnp.sum(total, axis=1, keepdims=True)
        both = jnp.where(low, pltpu.roll(mixed[:BLOCK], HEAD, 1), mixed[BLOCK:])
        attn[core, i] = jnp.where(i < live[0], both, 0.0).astype(BF16)
        attn_copy(i).start()

    def project(i):
        attn_got(i).wait_recv()
        for d in near:
            cols = pl.ds(pl.multiple_of((ahead(d) * 2 + core) * BLOCK, BLOCK), BLOCK)
            term = jnp.dot(attn[0, i], ow[0, :, cols], preferred_element_type=F32)
            term += jnp.dot(attn[1, i], ow[1, :, cols], preferred_element_type=F32)
            if d == 0:
                part_own[i] = term
            else:
                part[i, d - 1] = term.astype(BF16)
                part_copy(i, d).start()

    def step(i, _):
        attend(i)

        @pl.when(i > 0)
        def _():
            project(i - 1)

        return 0

    lax.fori_loop(0, qblocks, step, 0)
    project(qblocks - 1)

    def finish(i, _):
        term = part_own[i]
        for d in far:
            part_copy(i, d).wait_recv()
            term += got[i, d - 1].astype(F32)
        out[pl.ds(pl.multiple_of(i * BLOCK, BLOCK), BLOCK), :] = term.astype(BF16)
        return 0

    lax.fori_loop(0, qblocks, finish, 0)

    ow_copy.wait_send()
    for j in range(CHUNKS):
        for d in near:
            mold_c_copy(j, d).wait_send()
            kv_sib(j, d).wait_send()
            kv_x(j, d).wait_send()
            for slot in range(3):
                kv_core(slot, j, d).wait_send()
        for d in far:
            mold_z_copy(j, d).wait_send()
            kv_z_copy(j, d).wait_send()
    for d in far:
        q_z_copy(d).wait_send()
    for d in near:
        q_core(d).wait_send()
    for i in range(qblocks):
        attn_copy(i).wait_send()
        for d in far:
            part_copy(i, d).wait_send()


def solution(mesh):
    regions, shards = mesh.shape["region"], mesh.shape["wshard"]
    chips = shards // 2

    def step(queries, mold, q_weight, k_weight, v_weight, o_weight, lists, live):
        rows_q, feats = queries.shape
        rows_m = mold.shape[0]
        width, kv_cols = k_weight.shape
        qblocks, listed = lists.shape
        pool_blocks = rows_m // BLOCK
        rows_j = rows_m // chips // CHUNKS
        half = rows_j // 2
        piece = half // BLOCK
        far = chips - 1
        dma = pltpu.SemaphoreType.DMA
        any_space = pl.BlockSpec(memory_space=pl.ANY)
        smem = pl.BlockSpec(memory_space=pltpu.SMEM)
        scratch = [
            pltpu.VMEM((rows_q, feats), BF16),
            pltpu.VMEM((shards, rows_q, feats), BF16),
            pltpu.VMEM(q_weight.shape, BF16),
            pltpu.VMEM(k_weight.shape, BF16),
            pltpu.VMEM(v_weight.shape, BF16),
            pltpu.VMEM((width, 2 * kv_cols), BF16),
            pltpu.VMEM((2,) + o_weight.shape, BF16),
            pltpu.VMEM((rows_m // chips, feats), BF16),
            pltpu.VMEM((CHUNKS, far, rows_j, feats), BF16),
            pltpu.VMEM((CHUNKS, chips, half, feats), BF16),
            pltpu.VMEM((CHUNKS, KV_HEADS, piece, BLOCK, 2 * HEAD), BF16),
            pltpu.VMEM((3 * pool_blocks, BLOCK, 2 * HEAD), BF16),
            pltpu.VMEM((listed * BLOCK, 2 * HEAD), BF16),
            pltpu.VMEM((qblocks, 2 * BLOCK, 2 * HEAD), BF16),
            pltpu.VMEM((2 * BLOCK, listed * BLOCK), F32),
            pltpu.SMEM((qblocks, listed), F32),
            pltpu.VMEM((2, qblocks, BLOCK, 2 * HEAD), BF16),
            pltpu.VMEM((qblocks, far, BLOCK, feats), BF16),
            pltpu.VMEM((qblocks, BLOCK, feats), F32),
            pltpu.VMEM((qblocks, far, BLOCK, feats), BF16),
            dma((6,)),
        ]
        for shape in (
            (CHUNKS, far),
            (CHUNKS, chips),
            (CHUNKS, far),
            (3, CHUNKS, chips),
            (CHUNKS, chips),
            (CHUNKS, chips),
            (far,),
            (chips,),
            (),
            (qblocks,),
            (qblocks, far),
        ):
            scratch += [dma(shape), dma(shape)]
        return pl.pallas_call(
            functools.partial(kernel, chips, regions),
            out_shape=jax.ShapeDtypeStruct((rows_q, feats), BF16),
            in_specs=[any_space] * 6 + [smem] * 2,
            out_specs=pl.BlockSpec(memory_space=pltpu.VMEM),
            scratch_shapes=scratch,
            compiler_params=pltpu.CompilerParams(
                collective_id=0, has_side_effects=True, vmem_limit_bytes=40 << 20
            ),
        )(queries, mold, q_weight, k_weight, v_weight, o_weight, lists, live)

    return jax.shard_map(
        step,
        mesh=mesh,
        in_specs=(
            P("region", "wshard"),
            P("region", "wshard"),
            P(None, "wshard"),
            P(),
            P(),
            P("wshard", None),
            P("region", None),
            P("region"),
        ),
        out_specs=P("region", "wshard"),
        check_vma=False,
    )
```

time: 171 us -> 80.4 us (0.47)
  waiting for transfers between devices: 124 us -> 0 us
  Pallas kernels: 0 us -> 72.1 us
  between operations: 13.9 us -> 0.67 us
  matrix products: 10.3 us -> 0 us
  local copies, waits for them, and re-layouts: 13.3 us -> 7.26 us
  starting transfers between devices: 5.39 us -> 0 us
  other arithmetic: 3.23 us -> 0 us
    all_gather x2 -> x0, waiting for transfers between devices: 84.4 us -> none  [the longest x1 59.2 us: shards(): lax.all_gather(mold, 'wshard', axis=1, tiled=True)]
    pallas_call x0 -> x1, Pallas kernels: none -> 72.1 us  [step(): pl.pallas_call(functools.partial(kernel, chips, regions), out_shape=jax.S...]
    unnamed x4 -> x0, waiting for transfers between devices: 39.2 us -> none
    dot_general x5 -> x0, matrix products: 10.3 us -> none  [the longest x1 3.9 us: shards(): jnp.dot(lax.all_gather(mold, 'wshard', axis=1, tiled=True), rows_w, prefe...]
    ppermute x2 -> x0, starting transfers between devices: 5.31 us -> none  [the longest x1 4.02 us: padded(): lax.ppermute(lax.slice_in_dim(block, block.shape[dim] - width, None, axis...]
    gather x2 -> x0, local copies, waits for them, and re-layouts: 3.93 us -> none  [shards(): fetched = jnp.take(key_pool, local_ids, axis=0)]
    unnamed x9 -> x15, local copies, waits for them, and re-layouts: 3.47 us -> 7.26 us
    another operation x2 -> x0, local copies, waits for them, and re-layouts: 2.12 us -> none
  transfers between devices with their start and end apart: 5 -> 0, of which waited for: 3 -> 0; matrix products, arithmetic and copies ran while one was open for 6% -> 0% of each run, Pallas kernels for 0% -> 0%
where the time goes in v1:
time: 80.4 us; the launch traced here: 80 us
  Pallas kernels  72.1 us (90%)
  local copies, waits for them, and re-layouts  7.26 us (9%)
    pallas_call x1, Pallas kernels, step(): pl.pallas_call(functools.partial(kernel, chips, regions), out_shape=jax.S...  72.1 us
    unnamed x15, local copies, waits for them, and re-layouts  7.26 us

profile of v1, /device:TPU:1, one launch (start us, length us, event | category | flops | bytes accessed | tf_op | source)
XLA Modules:
  0.0 80.0 jit_solution(15427114963551933032)
XLA Ops:
  0.7 0.0 copy-start
  0.7 1.0 %copy-done = bf16[2048,128]{1,0:T(8,128)(2,1)S(1)} copy-done((bf16[2048,128]{1,0:T(8,128)(2,1)S(1)}, bf16[2048,128]{1,0:T(8,128)(2,1)}, u32[]{:S(2)}) %copy-start) | copy-done | bytes 524312
  1.7 0.0 copy-start.1
  1.7 1.0 %copy-done.1 = bf16[1024,256]{1,0:T(8,128)(2,1)S(1)} copy-done((bf16[1024,256]{1,0:T(8,128)(2,1)S(1)}, bf16[1024,256]{1,0:T(8,128)(2,1)}, u32[]{:S(2)}) %copy-start.1) | copy-done | bytes 524312
  2.7 0.0 copy-start.2
  2.7 1.0 %copy-done.2 = bf16[1024,256]{1,0:T(8,128)(2,1)S(1)} copy-done((bf16[1024,256]{1,0:T(8,128)(2,1)S(1)}, bf16[1024,256]{1,0:T(8,128)(2,1)}, u32[]{:S(2)}) %copy-start.2) | copy-done | bytes 524312
  3.8 0.0 copy-start.3
  3.8 0.9 %copy-done.3 = bf16[1024,128]{1,0:T(8,128)(2,1)S(1)} copy-done((bf16[1024,128]{1,0:T(8,128)(2,1)S(1)}, bf16[1024,128]{1,0:T(8,128)(2,1)}, u32[]{:S(2)}) %copy-start.3) | copy-done | bytes 262168
  4.7 0.0 copy-start.4
  4.7 0.9 %copy-done.4 = bf16[128,1024]{1,0:T(8,128)(2,1)S(1)} copy-done((bf16[128,1024]{1,0:T(8,128)(2,1)S(1)}, bf16[128,1024]{1,0:T(8,128)(2,1)}, u32[]{:S(2)}) %copy-start.4) | copy-done | bytes 262168
  5.7 0.0 copy-start.5
  5.7 0.9 %copy-done.5 = bf16[512,128]{1,0:T(8,128)(2,1)S(1)} copy-done((bf16[512,128]{1,0:T(8,128)(2,1)S(1)}, bf16[512,128]{1,0:T(8,128)(2,1)}, u32[]{:S(2)}) %copy-start.5) | copy-done | bytes 131096
  6.6 0.0 copy-start.6
  6.6 0.7 copy-done.6
  7.3 72.1 %shard_map.82 = bf16[512,128]{1,0:T(8,128)(2,1)S(1)} custom-call(bf16[512,128]{1,0:T(8,128)(2,1)S(1)} %copy-done.5, bf16[2048,128]{1,0:T(8,128)(2,1)S(1)} %copy-done, bf16[1024,128]{1,0:T(8,128)(2,1)S(1)} %copy-done.3, bf16[1024,256]{1,0:T(8,128)(2,1)S(1)} %copy-done.1, bf16[1024,256]{1,0:T(8,128)(2,1)S(1)} %copy-done.2, bf16[128,1024]{1,0:T(8,128)(2,1)S(1)} %copy-done.4, ...), custom_call_target="tpu_custom_call" | custom-call | tf_op jit(solution)/shard_map/pallas_call | solution.py:448
  79.4 0.7 copy.11
Async XLA Ops:
  0.7 1.0 %copy-start = (bf16[2048,128]{1,0:T(8,128)(2,1)S(1)}, bf16[2048,128]{1,0:T(8,128)(2,1)}, u32[]{:S(2)}) copy-start(bf16[2048,128]{1,0:T(8,128)(2,1)} %mold.1) | copy-start | bytes 1572868
  1.7 1.0 %copy-start.1 = (bf16[1024,256]{1,0:T(8,128)(2,1)S(1)}, bf16[1024,256]{1,0:T(8,128)(2,1)}, u32[]{:S(2)}) copy-start(bf16[1024,256]{1,0:T(8,128)(2,1)} %k_weight.1) | copy-start | bytes 1572868
  2.7 1.0 %copy-start.2 = (bf16[1024,256]{1,0:T(8,128)(2,1)S(1)}, bf16[1024,256]{1,0:T(8,128)(2,1)}, u32[]{:S(2)}) copy-start(bf16[1024,256]{1,0:T(8,128)(2,1)} %v_weight.1) | copy-start | bytes 1572868
  3.8 0.9 %copy-start.3 = (bf16[1024,128]{1,0:T(8,128)(2,1)S(1)}, bf16[1024,128]{1,0:T(8,128)(2,1)}, u32[]{:S(2)}) copy-start(bf16[1024,128]{1,0:T(8,128)(2,1)} %q_weight.1) | copy-start | bytes 786436
  4.7 0.9 %copy-start.4 = (bf16[128,1024]{1,0:T(8,128)(2,1)S(1)}, bf16[128,1024]{1,0:T(8,128)(2,1)}, u32[]{:S(2)}) copy-start(bf16[128,1024]{1,0:T(8,128)(2,1)} %o_weight.1) | copy-start | bytes 786436
  5.7 0.9 %copy-start.5 = (bf16[512,128]{1,0:T(8,128)(2,1)S(1)}, bf16[512,128]{1,0:T(8,128)(2,1)}, u32[]{:S(2)}) copy-start(bf16[512,128]{1,0:T(8,128)(2,1)} %queries.1) | copy-start | bytes 393220
  6.6 0.7 copy-start.6

commit v2 on v1

v2 whole, which is shorter than its diff:
```python
import functools

import jax
import jax.numpy as jnp
from jax import lax
from jax.experimental import pallas as pl
from jax.experimental.pallas import tpu as pltpu
from jax.sharding import PartitionSpec as P

HEAD = 64
KV_HEADS = 4
BLOCK = 128
MESH = pl.DeviceIdType.MESH
CHUNKS = 2
F32, BF16 = jnp.float32, jnp.bfloat16


def kernel(
    chips,
    regions,
    queries,
    mold,
    q_weight,
    k_weight,
    v_weight,
    o_weight,
    lists,
    live,
    out,
    q_feats,
    q_rows,
    q_send,
    qw,
    qwz,
    kw,
    vw,
    wkv,
    ow,
    mold_own,
    mold_z,
    mold_c,
    kv_send,
    pool,
    kv_list,
    q_ext,
    scores,
    bias,
    owz,
    attn,
    attn_got,
    part,
    part_got,
    out_send,
    sem_local,
    mz_s,
    mz_r,
    mc_s,
    mc_r,
    kz_s,
    kz_r,
    kc_s,
    kc_r,
    ki_s,
    ki_r,
    kx_s,
    kx_r,
    qz_s,
    qz_r,
    qc_s,
    qc_r,
    qh_s,
    qh_r,
    w1_s,
    w1_r,
    w2_s,
    w2_r,
    w3_s,
    w3_r,
    o1_s,
    o1_r,
    o2_s,
    o2_r,
    o3_s,
    o3_r,
    az_s,
    az_r,
    pc_s,
    pc_r,
    oz_s,
    oz_r,
):
    region = lax.axis_index("region")
    shard = lax.axis_index("wshard")
    chip = shard // 2
    core = lax.rem(shard, 2)
    other = 1 - core
    odd = lax.rem(region, 2)
    qblocks, listed = lists.shape
    pool_blocks = pool.shape[0] // 3
    chip_blocks = pool_blocks // chips
    chip_rows = chip_blocks * BLOCK
    rows_j = chip_rows // CHUNKS
    half = rows_j // 2
    piece = half // BLOCK
    far = range(1, chips)
    near = range(chips)

    def ahead(d):
        return lax.rem(chip + d, chips)

    def behind(d):
        return lax.rem(chip + chips - d, chips)

    def z_peer(d):
        return (region, ahead(d) * 2 + core)

    core_peer = (region, chip * 2 + other)
    sibling = (region + 1 - 2 * odd, shard)
    x_to = (lax.rem(region + regions + 2 - 4 * odd, regions), shard)
    x_from = (lax.rem(region + regions - 2 + 4 * odd, regions), shard)
    column = region // 2
    side_x = 4
    side_y = regions // 2 // side_x
    at_x = lax.rem(column, side_x)
    at_y = column // side_x
    share = qwz.shape[2]
    step_s = 1 + 2 * odd
    offsets = (0, step_s, chips - step_s, 2)

    def x_peer(e):
        return ((at_y * side_x + lax.rem(at_x + e, side_x)) * 2 + odd, shard)

    def y_peer(e):
        return ((lax.rem(at_y + e, side_y) * side_x + at_x) * 2 + odd, shard)

    def sib_peer(d):
        return (sibling[0], ahead(d) * 2 + core)

    def remote(src, dst, send, recv, peer):
        return pltpu.make_async_remote_copy(
            src_ref=src, dst_ref=dst, send_sem=send, recv_sem=recv, device_id=peer, device_id_type=MESH
        )

    local = [
        pltpu.make_async_copy(k_weight, kw, sem_local.at[0]),
        pltpu.make_async_copy(v_weight, vw, sem_local.at[1]),
        pltpu.make_async_copy(q_weight, qw, sem_local.at[2]),
        pltpu.make_async_copy(o_weight, ow, sem_local.at[3]),
        pltpu.make_async_copy(
            queries.at[pl.ds(pl.multiple_of(chip * BLOCK, BLOCK), BLOCK)], q_feats.at[shard], sem_local.at[4]
        ),
        pltpu.make_async_copy(
            mold.at[pl.ds(pl.multiple_of(chip * chip_rows, BLOCK), chip_rows)], mold_own, sem_local.at[5]
        ),
    ]
    for copy in (local[5], local[0], local[1], local[4], local[2], local[3]):
        copy.start()

    barrier = pltpu.get_barrier_semaphore()
    partners = [z_peer(d) for d in far] + [core_peer, sibling, x_to, x_from]
    partners += [sib_peer(chips - step_s), sib_peer(2)]
    partners += [x_peer(e) for e in range(1, side_x)] + [y_peer(e) for e in range(1, side_y)]
    for peer in partners:
        pl.semaphore_signal(barrier, inc=1, device_id=peer, device_id_type=MESH)
    pl.semaphore_wait(barrier, len(partners))

    def w1_copy(d):
        rows = pl.ds(pl.multiple_of(column * share, share), share)
        return remote(q_weight.at[rows], qwz.at[column, d - 1], w1_s.at[d - 1], w1_r.at[d - 1], z_peer(d))

    def w2_copy(e, sent):
        spot = column if sent else at_y * side_x + lax.rem(at_x + side_x - e, side_x)
        return remote(qwz.at[column], qwz.at[spot], w2_s.at[e - 1], w2_r.at[e - 1], x_peer(e))

    def w3_copy(e, sent):
        mine = pl.ds(at_y * side_x, side_x)
        spot = mine if sent else pl.ds(lax.rem(at_y + side_y - e, side_y) * side_x, side_x)
        return remote(qwz.at[mine], qwz.at[spot], w3_s.at[e - 1], w3_r.at[e - 1], y_peer(e))

    column_o = at_x * side_y + at_y

    def o1_copy(d):
        rows = pl.ds(pl.multiple_of(lax.rem(column_o, 2) * share, share), share)
        cols = pl.ds(pl.multiple_of(column_o // 2 * BLOCK, BLOCK), BLOCK)
        return remote(o_weight.at[rows, cols], owz.at[column_o, d - 1], o1_s.at[d - 1], o1_r.at[d - 1], z_peer(d))

    def o2_copy(e, sent):
        spot = column_o if sent else at_x * side_y + lax.rem(at_y + side_y - e, side_y)
        return remote(owz.at[column_o], owz.at[spot], o2_s.at[e - 1], o2_r.at[e - 1], y_peer(e))

    def o3_copy(e, sent):
        mine = pl.ds(at_x * side_y, side_y)
        spot = mine if sent else pl.ds(lax.rem(at_x + side_x - e, side_x) * side_y, side_y)
        return remote(owz.at[mine], owz.at[spot], o3_s.at[e - 1], o3_r.at[e - 1], x_peer(e))

    for d in far:
        w1_copy(d).start()
    for d in far:
        o1_copy(d).start()

    def mold_z_copy(j, d):
        row = pl.multiple_of(ahead(d) * chip_rows + j * rows_j, BLOCK)
        return remote(
            mold.at[pl.ds(row, rows_j)], mold_z.at[j, d - 1], mz_s.at[j, d - 1], mz_r.at[j, d - 1], z_peer(d)
        )

    for j in range(CHUNKS):
        for d in far:
            mold_z_copy(j, d).start()

    def mold_src(j, d, side):
        rows = pl.ds(pl.multiple_of(side * half, BLOCK), half)
        if d == 0:
            return mold_own.at[pl.ds(pl.multiple_of(j * rows_j + side * half, BLOCK), half)]
        return mold_z.at[j, d - 1, rows]

    def mold_c_copy(j, d):
        return remote(mold_src(j, d, other), mold_c.at[j, d], mc_s.at[j, d], mc_r.at[j, d], core_peer)

    local[5].wait()
    for j in range(CHUNKS):
        mold_c_copy(j, 0).start()

    local[0].wait()
    local[1].wait()
    for h in range(KV_HEADS):
        cols = slice(h * HEAD, (h + 1) * HEAD)
        wkv[:, h * 2 * HEAD : (h + 1) * 2 * HEAD] = jnp.concatenate([kw[:, cols], vw[:, cols]], axis=1)

    def mark(i, _):
        for l in range(listed):
            repeat = jnp.int32(0)
            for e in range(l):
                repeat = jnp.where(lists[i, e] == lists[i, l], jnp.int32(1), repeat)
            bias[i, l] = jnp.where(repeat == 1, F32(-1e30), F32(0.0))
        return 0

    lax.fori_loop(0, qblocks, mark, 0)

    def at_piece(slot, j, off, side):
        return pl.ds(slot * pool_blocks + behind(off) * chip_blocks + (j * 2 + side) * piece, piece)

    z_routes = ((step_s, 0), (chips - step_s, 1), (2, 1))
    z_arrivals = ((0, 1), (1, 1), (1, 3))

    def kv_z_copy(j, t):
        d, slot = z_routes[t]
        peer = sib_peer(d) if slot else z_peer(d)
        spot = at_piece(slot, j, 0, core)
        return remote(kv_send.at[j, ahead(d)], pool.at[spot], kz_s.at[j, t], kz_r.at[j, t], peer)

    def kv_z_got(j, t):
        slot, at = z_arrivals[t]
        spot = at_piece(slot, j, offsets[at], core)
        return remote(kv_send.at[j, 0], pool.at[spot], kz_s.at[j, t], kz_r.at[j, t], sibling)

    def kv_core(slot, j, t):
        spot = at_piece(slot, j, offsets[t], core)
        return remote(pool.at[spot], pool.at[spot], kc_s.at[slot, j, t], kc_r.at[slot, j, t], core_peer)

    def kv_core_got(slot, j, t):
        spot = at_piece(slot, j, offsets[t], other)
        return remote(pool.at[spot], pool.at[spot], kc_s.at[slot, j, t], kc_r.at[slot, j, t], core_peer)

    sib_sent = ((0, 0), (0, 1), (1, 1), (1, 3))
    sib_arrivals = ((1, 0), (1, 2), (0, 2), (0, 3))

    def kv_sib(j, t):
        slot, at = sib_sent[t]
        src = at_piece(slot, j, offsets[at], core)
        dst = at_piece(1 - slot, j, offsets[at], core)
        return remote(pool.at[src], pool.at[dst], ki_s.at[j, t], ki_r.at[j, t], sibling)

    def kv_sib_got(j, t):
        slot, at = sib_arrivals[t]
        spot = at_piece(slot, j, offsets[at], core)
        return remote(pool.at[spot], pool.at[spot], ki_s.at[j, t], ki_r.at[j, t], sibling)

    def kv_x(j, t):
        return remote(
            pool.at[at_piece(1, j, offsets[t], core)],
            pool.at[at_piece(2, j, offsets[t], core)],
            kx_s.at[j, t],
            kx_r.at[j, t],
            x_to,
        )

    def q_z_copy(d):
        rows = pl.ds(pl.multiple_of(ahead(d) * BLOCK, BLOCK), BLOCK)
        return remote(queries.at[rows], q_feats.at[shard], qz_s.at[d - 1], qz_r.at[d - 1], z_peer(d))

    def q_z_got(d):
        return remote(q_send.at[0], q_feats.at[behind(d) * 2 + core], qz_s.at[d - 1], qz_r.at[d - 1], z_peer(d))

    def q_core(d):
        spot = q_feats.at[behind(d) * 2 + core]
        return remote(spot, spot, qc_s.at[d], qc_r.at[d], core_peer)

    def q_core_got(d):
        spot = q_feats.at[behind(d) * 2 + other]
        return remote(spot, spot, qc_s.at[d], qc_r.at[d], core_peer)

    def q_heads(d):
        return remote(q_send.at[d - 1], q_rows.at[chip], qh_s.at[d - 1], qh_r.at[d - 1], z_peer(d))

    def q_heads_got(d):
        return remote(q_send.at[d - 1], q_rows.at[behind(d)], qh_s.at[d - 1], qh_r.at[d - 1], z_peer(d))

    local[4].wait()
    q_core(0).start()
    for d in far:
        w1_copy(d).wait_recv()
    for e in range(1, side_x):
        w2_copy(e, True).start()
    for d in far:
        o1_copy(d).wait_recv()
    for e in range(1, side_y):
        o2_copy(e, True).start()
    for e in range(1, side_x):
        w2_copy(e, False).wait_recv()
    for e in range(1, side_y):
        w3_copy(e, True).start()
    for e in range(1, side_y):
        o2_copy(e, False).wait_recv()
    for e in range(1, side_x):
        o3_copy(e, True).start()

    for j in range(CHUNKS):
        for d in far:
            mold_z_copy(j, d).wait_recv()
            mold_c_copy(j, d).start()
        total = jnp.zeros((half, wkv.shape[1]), F32)
        for d in near:
            depth = 2 * BLOCK
            base = pl.multiple_of(behind(d) * depth, depth)
            mine = wkv[pl.ds(pl.multiple_of(base + core * BLOCK, BLOCK), BLOCK), :]
            total += jnp.dot(mold_src(j, d, core)[...], mine, preferred_element_type=F32)
            mold_c_copy(j, d).wait_recv()
            theirs = wkv[pl.ds(pl.multiple_of(base + other * BLOCK, BLOCK), BLOCK), :]
            total += jnp.dot(mold_c[j, d], theirs, preferred_element_type=F32)
        pairs = total.astype(BF16)
        for h in range(KV_HEADS):
            kv_send[j, h] = pairs[:, h * BLOCK : (h + 1) * BLOCK].reshape(piece, BLOCK, BLOCK)
        pool[at_piece(0, j, 0, core)] = kv_send[j, chip]
        for t in range(3):
            kv_z_copy(j, t).start()
        kv_sib(j, 0).start()
        kv_core(0, j, 0).start()
        if j == 0:
            for d in far:
                q_z_copy(d).start()

    def forward(j):
        for t in range(3):
            kv_z_got(j, t).wait_recv()
            slot, at = z_arrivals[t]
            kv_sib(j, t + 1).start()
            if slot == 1:
                kv_x(j, at).start()
            kv_core(slot, j, at).start()

    forward(0)

    local[2].wait()
    for d in far:
        q_z_got(d).wait_recv()
        q_core(d).start()
    for e in range(1, side_y):
        w3_copy(e, False).wait_recv()
    for d in near:
        q_core_got(d).wait_recv()
    feats = jnp.concatenate([q_feats[f] for f in range(q_feats.shape[0])], axis=1)

    def project_q(weight):
        value = jnp.dot(feats, weight, preferred_element_type=F32).astype(BF16)
        return (value.astype(F32) * HEAD**-0.5).astype(BF16)

    for d in far:
        q_send[d - 1] = project_q(qwz[:, chips - d - 1].reshape(qw.shape))
        q_heads(d).start()
    q_rows[chip] = project_q(qw[...])

    for j in range(1, CHUNKS):
        forward(j)
    for j in range(CHUNKS):
        for t in range(4):
            kv_sib_got(j, t).wait_recv()
            slot, at = sib_arrivals[t]
            if slot == 1:
                kv_x(j, at).start()
            kv_core(slot, j, at).start()

    lane = lax.broadcasted_iota(jnp.int32, (BLOCK, 2 * HEAD), 1)
    for d in far:
        q_heads_got(d).wait_recv()
    for i in range(qblocks):
        value = q_rows[i].astype(F32)
        q_ext[i, :BLOCK] = jnp.where(lane < HEAD, value, 0.0).astype(BF16)
        q_ext[i, BLOCK:] = jnp.where(lane < HEAD, pltpu.roll(value, HEAD, 1), 0.0).astype(BF16)

    for j in range(CHUNKS):
        for t in (1, 3, 0, 2):
            kv_x(j, t).wait_recv()
            kv_core(2, j, t).start()

    for slot in range(3):
        for j in range(CHUNKS):
            for d in near:
                kv_core_got(slot, j, d).wait_recv()
    for e in range(1, side_x):
        o3_copy(e, False).wait_recv()
    local[3].wait()

    low = lax.broadcasted_iota(jnp.int32, (BLOCK, 2 * HEAD), 1) < HEAD
    wide = 2 * BLOCK

    def attn_copy(t):
        return remote(attn.at[t], attn_got.at[t - 1], az_s.at[t - 1], az_r.at[t - 1], z_peer(t))

    part_copy = remote(part, part_got, pc_s, pc_r, core_peer)

    def out_copy(d):
        rows = pl.ds(pl.multiple_of(chip * BLOCK, BLOCK), BLOCK)
        return remote(out_send.at[d - 1], out.at[rows], oz_s.at[d - 1], oz_r.at[d - 1], z_peer(d))

    def out_got(d):
        rows = pl.ds(pl.multiple_of(behind(d) * BLOCK, BLOCK), BLOCK)
        return remote(out_send.at[d - 1], out.at[rows], oz_s.at[d - 1], oz_r.at[d - 1], z_peer(d))

    def attend(t):
        i = ahead(t)
        for l in range(listed):
            block = lists[i, l]
            home = block // pool_blocks
            slot = jnp.where(home == region, 0, jnp.where(home == sibling[0], 1, 2))
            kv_list[l * BLOCK : (l + 1) * BLOCK] = pool[slot * pool_blocks + lax.rem(block, pool_blocks)]
        q = q_ext[i]
        top = jnp.full((wide, BLOCK), -jnp.inf, F32)
        for p in range(listed // 2):
            keys = kv_list[p * wide : (p + 1) * wide]
            s = lax.dot_general(q, keys, (((1,), (1,)), ((), ())), preferred_element_type=F32)
            for e in range(2):
                se = s[:, e * BLOCK : (e + 1) * BLOCK] + bias[i, 2 * p + e]
                scores[:, p * wide + e * BLOCK : p * wide + (e + 1) * BLOCK] = se
                top = jnp.maximum(top, se)
        top = jnp.max(top, axis=1, keepdims=True)
        total = jnp.zeros((wide, BLOCK), F32)
        mixed = jnp.zeros((wide, BLOCK), F32)
        for p in range(listed // 2):
            e = jnp.exp(scores[:, p * wide : (p + 1) * wide] - top)
            total += e[:, :BLOCK] + e[:, BLOCK:]
            mixed += jnp.dot(e.astype(BF16), kv_list[p * wide : (p + 1) * wide], preferred_element_type=F32)
        mixed = mixed / jnp.sum(total, axis=1, keepdims=True)
        both = jnp.where(low, pltpu.roll(mixed[:BLOCK], HEAD, 1), mixed[BLOCK:])
        attn[t] = jnp.where(i < live[0], both, 0.0).astype(BF16)

    def step(u, _):
        t = lax.rem(u + 1, chips)
        attend(t)

        @pl.when(u < chips - 1)
        def _():
            attn_copy(t).start()

        return 0

    lax.fori_loop(0, qblocks, step, 0)

    for d in far:
        attn_copy(d).wait_recv()
    heads = jnp.concatenate([attn[0]] + [attn_got[d - 1] for d in far], axis=1)

    def project(block):
        cols = pl.ds(pl.multiple_of(block * BLOCK, BLOCK), BLOCK)
        weight = jnp.concatenate(
            [ow[:, cols]] + [owz[pl.ds(block * 2, 2), d - 1].reshape(BLOCK, BLOCK) for d in far], axis=0
        )
        return jnp.dot(heads, weight, preferred_element_type=F32)

    for d in near:
        part[d] = project(ahead(d) * 2 + other).astype(BF16)
    part_copy.start()
    terms = [project(ahead(d) * 2 + core) for d in near]
    part_copy.wait_recv()
    for d in far:
        out_send[d - 1] = (terms[d] + part_got[d].astype(F32)).astype(BF16)
        out_copy(d).start()
    rows = pl.ds(pl.multiple_of(chip * BLOCK, BLOCK), BLOCK)
    out[rows, :] = (terms[0] + part_got[0].astype(F32)).astype(BF16)
    for d in far:
        out_got(d).wait_recv()

    part_copy.wait_send()
    for d in far:
        attn_copy(d).wait_send()
        out_copy(d).wait_send()
        o1_copy(d).wait_send()
    for e in range(1, side_y):
        o2_copy(e, True).wait_send()
    for e in range(1, side_x):
        o3_copy(e, True).wait_send()
    for j in range(CHUNKS):
        for d in near:
            mold_c_copy(j, d).wait_send()
            kv_sib(j, d).wait_send()
            kv_x(j, d).wait_send()
            for slot in range(3):
                kv_core(slot, j, d).wait_send()
        for d in far:
            mold_z_copy(j, d).wait_send()
        for t in range(3):
            kv_z_copy(j, t).wait_send()
    for d in far:
        w1_copy(d).wait_send()
        q_z_copy(d).wait_send()
        q_heads(d).wait_send()
    for e in range(1, side_x):
        w2_copy(e, True).wait_send()
    for e in range(1, side_y):
        w3_copy(e, True).wait_send()
    for d in near:
        q_core(d).wait_send()


def solution(mesh):
    regions, shards = mesh.shape["region"], mesh.shape["wshard"]
    chips = shards // 2

    def step(queries, mold, q_weight, k_weight, v_weight, o_weight, lists, live):
        rows_q, feats = queries.shape
        rows_m = mold.shape[0]
        width, kv_cols = k_weight.shape
        qblocks, listed = lists.shape
        pool_blocks = rows_m // BLOCK
        rows_j = rows_m // chips // CHUNKS
        half = rows_j // 2
        piece = half // BLOCK
        far = chips - 1
        columns = regions // 2
        dma = pltpu.SemaphoreType.DMA
        any_space = pl.BlockSpec(memory_space=pl.ANY)
        smem = pl.BlockSpec(memory_space=pltpu.SMEM)
        scratch = [
            pltpu.VMEM((shards, BLOCK, feats), BF16),
            pltpu.VMEM((chips, BLOCK, feats), BF16),
            pltpu.VMEM((far, BLOCK, feats), BF16),
            pltpu.VMEM(q_weight.shape, BF16),
            pltpu.VMEM((columns, far, width // columns, feats), BF16),
            pltpu.VMEM(k_weight.shape, BF16),
            pltpu.VMEM(v_weight.shape, BF16),
            pltpu.VMEM((width, 2 * kv_cols), BF16),
            pltpu.VMEM(o_weight.shape, BF16),
            pltpu.VMEM((rows_m // chips, feats), BF16),
            pltpu.VMEM((CHUNKS, far, rows_j, feats), BF16),
            pltpu.VMEM((CHUNKS, chips, half, feats), BF16),
            pltpu.VMEM((CHUNKS, KV_HEADS, piece, BLOCK, 2 * HEAD), BF16),
            pltpu.VMEM((3 * pool_blocks, BLOCK, 2 * HEAD), BF16),
            pltpu.VMEM((listed * BLOCK, 2 * HEAD), BF16),
            pltpu.VMEM((qblocks, 2 * BLOCK, 2 * HEAD), BF16),
            pltpu.VMEM((2 * BLOCK, listed * BLOCK), F32),
            pltpu.SMEM((qblocks, listed), F32),
            pltpu.VMEM((columns, far, width // columns, feats), BF16),
            pltpu.VMEM((chips, BLOCK, 2 * HEAD), BF16),
            pltpu.VMEM((far, BLOCK, 2 * HEAD), BF16),
            pltpu.VMEM((chips, BLOCK, feats), BF16),
            pltpu.VMEM((chips, BLOCK, feats), BF16),
            pltpu.VMEM((far, BLOCK, feats), BF16),
            dma((6,)),
        ]
        for shape in (
            (CHUNKS, far),
            (CHUNKS, chips),
            (CHUNKS, 3),
            (3, CHUNKS, chips),
            (CHUNKS, chips),
            (CHUNKS, chips),
            (far,),
            (chips,),
            (far,),
            (far,),
            (3,),
            (regions // 8 - 1,),
            (far,),
            (regions // 8 - 1,),
            (3,),
            (far,),
            (),
            (far,),
        ):
            scratch += [dma(shape), dma(shape)]
        return pl.pallas_call(
            functools.partial(kernel, chips, regions),
            out_shape=jax.ShapeDtypeStruct((rows_q, feats), BF16),
            in_specs=[any_space] * 6 + [smem] * 2,
            out_specs=pl.BlockSpec(memory_space=pltpu.VMEM),
            scratch_shapes=scratch,
            compiler_params=pltpu.CompilerParams(
                collective_id=0, has_side_effects=True, vmem_limit_bytes=60 << 20
            ),
        )(queries, mold, q_weight, k_weight, v_weight, o_weight, lists, live)

    return jax.shard_map(
        step,
        mesh=mesh,
        in_specs=(
            P("region", "wshard"),
            P("region", "wshard"),
            P(None, "wshard"),
            P(),
            P(),
            P("wshard", None),
            P("region", None),
            P("region"),
        ),
        out_specs=P("region", "wshard"),
        check_vma=False,
    )
```

time: 80.4 us -> 65.2 us (0.81)
  Pallas kernels: 72.1 us -> 62.8 us
  local copies, waits for them, and re-layouts: 7.26 us -> 1.57 us
    pallas_call x1, Pallas kernels: 72.1 us -> 62.8 us  [step(): pl.pallas_call(functools.partial(kernel, chips, regions), out_shape=jax.S...]
    unnamed x15 -> x1, local copies, waits for them, and re-layouts: 7.26 us -> 1.57 us
where the time goes in v2:
time: 65.2 us; the launch traced here: 65.1 us
  Pallas kernels  62.8 us (96%)
  local copies, waits for them, and re-layouts  1.57 us (2%)
  between operations  0.66 us (1%)
    pallas_call x1, Pallas kernels, step(): pl.pallas_call(functools.partial(kernel, chips, regions), out_shape=jax.S...  62.8 us
    unnamed x1, local copies, waits for them, and re-layouts  1.57 us

profile of v2, /device:TPU:1, one launch (start us, length us, event | category | flops | bytes accessed | tf_op | source)
XLA Modules:
  0.0 65.1 jit_solution(7177925340649549890)
XLA Ops:
  0.7 62.8 %shard_map.82 = bf16[512,128]{1,0:T(8,128)(2,1)} custom-call(bf16[512,128]{1,0:T(8,128)(2,1)} %queries.1, bf16[2048,128]{1,0:T(8,128)(2,1)} %mold.1, bf16[1024,128]{1,0:T(8,128)(2,1)} %q_weight.1, bf16[1024,256]{1,0:T(8,128)(2,1)} %k_weight.1, bf16[1024,256]{1,0:T(8,128)(2,1)} %v_weight.1, bf16[128,1024]{1,0:T(8,128)(2,1)} %o_weight.1, s32[4,16]{1,0:T(4,128)} %lists.1, ...), custom_call_target="tpu_custom_call" | custom-call | tf_op jit(solution)/shard_map/pallas_call | solution.py:591
  63.5 1.6 %copy.11 = bf16[512,128]{1,0:T(8,128)(2,1)} copy(bf16[512,128]{1,0:T(8,128)(2,1)} %shard_map.82) | data formatting | bytes 262144

commit v3 on v2

--- a/solution.py
+++ b/solution.py
@@ -27,6 +27,7 @@
     lists,
     live,
     out,
+    q_own,
     q_feats,
     q_rows,
     q_send,
@@ -44,7 +45,7 @@
     kv_list,
     q_ext,
     scores,
-    bias,
+    keep,
     owz,
     attn,
     attn_got,
@@ -146,14 +147,10 @@
         pltpu.make_async_copy(v_weight, vw, sem_local.at[1]),
         pltpu.make_async_copy(q_weight, qw, sem_local.at[2]),
         pltpu.make_async_copy(o_weight, ow, sem_local.at[3]),
-        pltpu.make_async_copy(
-            queries.at[pl.ds(pl.multiple_of(chip * BLOCK, BLOCK), BLOCK)], q_feats.at[shard], sem_local.at[4]
-        ),
-        pltpu.make_async_copy(
-            mold.at[pl.ds(pl.multiple_of(chip * chip_rows, BLOCK), chip_rows)], mold_own, sem_local.at[5]
-        ),
+        pltpu.make_async_copy(queries, q_own, sem_local.at[4]),
+        pltpu.make_async_copy(mold, mold_own, sem_local.at[5]),
     ]
-    for copy in (local[5], local[0], local[1], local[4], local[2], local[3]):
+    for copy in (local[5], local[2], local[3], local[0], local[1], local[4]):
         copy.start()
 
     barrier = pltpu.get_barrier_semaphore()
@@ -162,67 +159,9 @@
     partners += [x_peer(e) for e in range(1, side_x)] + [y_peer(e) for e in range(1, side_y)]
     for peer in partners:
         pl.semaphore_signal(barrier, inc=1, device_id=peer, device_id_type=MESH)
-    pl.semaphore_wait(barrier, len(partners))
-
-    def w1_copy(d):
-        rows = pl.ds(pl.multiple_of(column * share, share), share)
-        return remote(q_weight.at[rows], qwz.at[column, d - 1], w1_s.at[d - 1], w1_r.at[d - 1], z_peer(d))
-
-    def w2_copy(e, sent):
-        spot = column if sent else at_y * side_x + lax.rem(at_x + side_x - e, side_x)
-        return remote(qwz.at[column], qwz.at[spot], w2_s.at[e - 1], w2_r.at[e - 1], x_peer(e))
-
-    def w3_copy(e, sent):
-        mine = pl.ds(at_y * side_x, side_x)
-        spot = mine if sent else pl.ds(lax.rem(at_y + side_y - e, side_y) * side_x, side_x)
-        return remote(qwz.at[mine], qwz.at[spot], w3_s.at[e - 1], w3_r.at[e - 1], y_peer(e))
-
-    column_o = at_x * side_y + at_y
-
-    def o1_copy(d):
-        rows = pl.ds(pl.multiple_of(lax.rem(column_o, 2) * share, share), share)
-        cols = pl.ds(pl.multiple_of(column_o // 2 * BLOCK, BLOCK), BLOCK)
-        return remote(o_weight.at[rows, cols], owz.at[column_o, d - 1], o1_s.at[d - 1], o1_r.at[d - 1], z_peer(d))
-
-    def o2_copy(e, sent):
-        spot = column_o if sent else at_x * side_y + lax.rem(at_y + side_y - e, side_y)
-        return remote(owz.at[column_o], owz.at[spot], o2_s.at[e - 1], o2_r.at[e - 1], y_peer(e))
-
-    def o3_copy(e, sent):
-        mine = pl.ds(at_x * side_y, side_y)
-        spot = mine if sent else pl.ds(lax.rem(at_x + side_x - e, side_x) * side_y, side_y)
-        return remote(owz.at[mine], owz.at[spot], o3_s.at[e - 1], o3_r.at[e - 1], x_peer(e))
-
-    for d in far:
-        w1_copy(d).start()
-    for d in far:
-        o1_copy(d).start()
-
-    def mold_z_copy(j, d):
-        row = pl.multiple_of(ahead(d) * chip_rows + j * rows_j, BLOCK)
-        return remote(
-            mold.at[pl.ds(row, rows_j)], mold_z.at[j, d - 1], mz_s.at[j, d - 1], mz_r.at[j, d - 1], z_peer(d)
-        )
-
-    for j in range(CHUNKS):
-        for d in far:
-            mold_z_copy(j, d).start()
-
-    def mold_src(j, d, side):
-        rows = pl.ds(pl.multiple_of(side * half, BLOCK), half)
-        if d == 0:
-            return mold_own.at[pl.ds(pl.multiple_of(j * rows_j + side * half, BLOCK), half)]
-        return mold_z.at[j, d - 1, rows]
-
-    def mold_c_copy(j, d):
-        return remote(mold_src(j, d, other), mold_c.at[j, d], mc_s.at[j, d], mc_r.at[j, d], core_peer)
-
-    local[5].wait()
-    for j in range(CHUNKS):
-        mold_c_copy(j, 0).start()
-
-    local[0].wait()
-    local[1].wait()
+    for copy in local:
+        copy.wait()
+    q_feats[shard] = q_own[pl.ds(pl.multiple_of(chip * BLOCK, BLOCK), BLOCK), :]
     for h in range(KV_HEADS):
         cols = slice(h * HEAD, (h + 1) * HEAD)
         wkv[:, h * 2 * HEAD : (h + 1) * 2 * HEAD] = jnp.concatenate([kw[:, cols], vw[:, cols]], axis=1)
@@ -232,10 +171,68 @@
             repeat = jnp.int32(0)
             for e in range(l):
                 repeat = jnp.where(lists[i, e] == lists[i, l], jnp.int32(1), repeat)
-            bias[i, l] = jnp.where(repeat == 1, F32(-1e30), F32(0.0))
+            keep[i, l] = jnp.where(repeat == 1, F32(0.0), F32(1.0))
         return 0
 
     lax.fori_loop(0, qblocks, mark, 0)
+
+    pl.semaphore_wait(barrier, len(partners))
+
+    def w1_copy(d):
+        rows = pl.ds(pl.multiple_of(column * share, share), share)
+        return remote(qw.at[rows], qwz.at[column, d - 1], w1_s.at[d - 1], w1_r.at[d - 1], z_peer(d))
+
+    def w2_copy(e, sent):
+        spot = column if sent else at_y * side_x + lax.rem(at_x + side_x - e, side_x)
+        return remote(qwz.at[column], qwz.at[spot], w2_s.at[e - 1], w2_r.at[e - 1], x_peer(e))
+
+    def w3_copy(e, sent):
+        mine = pl.ds(at_y * side_x, side_x)
+        spot = mine if sent else pl.ds(lax.rem(at_y + side_y - e, side_y) * side_x, side_x)
+        return remote(qwz.at[mine], qwz.at[spot], w3_s.at[e - 1], w3_r.at[e - 1], y_peer(e))
+
+    column_o = at_x * side_y + at_y
+
+    def o1_copy(d):
+        rows = pl.ds(pl.multiple_of(lax.rem(column_o, 2) * share, share), share)
+        cols = pl.ds(pl.multiple_of(column_o // 2 * BLOCK, BLOCK), BLOCK)
+        return remote(ow.at[rows, cols], owz.at[column_o, d - 1], o1_s.at[d - 1], o1_r.at[d - 1], z_peer(d))
+
+    def o2_copy(e, sent):
+        spot = column_o if sent else at_x * side_y + lax.rem(at_y + side_y - e, side_y)
+        return remote(owz.at[column_o], owz.at[spot], o2_s.at[e - 1], o2_r.at[e - 1], y_peer(e))
+
+    def o3_copy(e, sent):
+        mine = pl.ds(at_x * side_y, side_y)
+        spot = mine if sent else pl.ds(lax.rem(at_x + side_x - e, side_x) * side_y, side_y)
+        return remote(owz.at[mine], owz.at[spot], o3_s.at[e - 1], o3_r.at[e - 1], x_peer(e))
+
+    for d in far:
+        w1_copy(d).start()
+    for d in far:
+        o1_copy(d).start()
+
+    def mold_z_copy(j, d):
+        row = pl.multiple_of(ahead(d) * chip_rows + j * rows_j, BLOCK)
+        return remote(
+            mold_own.at[pl.ds(row, rows_j)], mold_z.at[j, d - 1], mz_s.at[j, d - 1], mz_r.at[j, d - 1], z_peer(d)
+        )
+
+    for j in range(CHUNKS):
+        for d in far:
+            mold_z_copy(j, d).start()
+
+    def mold_src(j, d, side):
+        rows = pl.ds(pl.multiple_of(side * half, BLOCK), half)
+        if d == 0:
+            return mold_own.at[pl.ds(pl.multiple_of(chip * chip_rows + j * rows_j + side * half, BLOCK), half)]
+        return mold_z.at[j, d - 1, rows]
+
+    def mold_c_copy(j, d):
+        return remote(mold_src(j, d, other), mold_c.at[j, d], mc_s.at[j, d], mc_r.at[j, d], core_peer)
+
+    for j in range(CHUNKS):
+        mold_c_copy(j, 0).start()
 
     def at_piece(slot, j, off, side):
         return pl.ds(slot * pool_blocks + behind(off) * chip_blocks + (j * 2 + side) * piece, piece)
@@ -287,7 +284,7 @@
 
     def q_z_copy(d):
         rows = pl.ds(pl.multiple_of(ahead(d) * BLOCK, BLOCK), BLOCK)
-        return remote(queries.at[rows], q_feats.at[shard], qz_s.at[d - 1], qz_r.at[d - 1], z_peer(d))
+        return remote(q_own.at[rows], q_feats.at[shard], qz_s.at[d - 1], qz_r.at[d - 1], z_peer(d))
 
     def q_z_got(d):
         return remote(q_send.at[0], q_feats.at[behind(d) * 2 + core], qz_s.at[d - 1], qz_r.at[d - 1], z_peer(d))
@@ -306,7 +303,6 @@
     def q_heads_got(d):
         return remote(q_send.at[d - 1], q_rows.at[behind(d)], qh_s.at[d - 1], qh_r.at[d - 1], z_peer(d))
 
-    local[4].wait()
     q_core(0).start()
     for d in far:
         w1_copy(d).wait_recv()
@@ -361,7 +357,6 @@
 
     forward(0)
 
-    local[2].wait()
     for d in far:
         q_z_got(d).wait_recv()
         q_core(d).start()
@@ -409,7 +404,6 @@
                 kv_core_got(slot, j, d).wait_recv()
     for e in range(1, side_x):
         o3_copy(e, False).wait_recv()
-    local[3].wait()
 
     low = lax.broadcasted_iota(jnp.int32, (BLOCK, 2 * HEAD), 1) < HEAD
     wide = 2 * BLOCK
@@ -427,44 +421,39 @@
         rows = pl.ds(pl.multiple_of(behind(d) * BLOCK, BLOCK), BLOCK)
         return remote(out_send.at[d - 1], out.at[rows], oz_s.at[d - 1], oz_r.at[d - 1], z_peer(d))
 
-    def attend(t):
+    ones = low.astype(F32).astype(BF16)
+    high = (1.0 - low.astype(F32)).astype(BF16)
+
+    def attend(t, buf):
         i = ahead(t)
         for l in range(listed):
             block = lists[i, l]
             home = block // pool_blocks
             slot = jnp.where(home == region, 0, jnp.where(home == sibling[0], 1, 2))
-            kv_list[l * BLOCK : (l + 1) * BLOCK] = pool[slot * pool_blocks + lax.rem(block, pool_blocks)]
+            rows = slice(l * BLOCK, (l + 1) * BLOCK)
+            pair = pool[slot * pool_blocks + lax.rem(block, pool_blocks)]
+            kv_list[buf, 0, rows] = pair
+            kv_list[buf, 1, rows] = (pair * high + ones) * jnp.full(pair.shape, keep[i, l], F32).astype(BF16)
         q = q_ext[i]
         top = jnp.full((wide, BLOCK), -jnp.inf, F32)
         for p in range(listed // 2):
-            keys = kv_list[p * wide : (p + 1) * wide]
+            keys = kv_list[buf, 0, p * wide : (p + 1) * wide]
             s = lax.dot_general(q, keys, (((1,), (1,)), ((), ())), preferred_element_type=F32)
-            for e in range(2):
-                se = s[:, e * BLOCK : (e + 1) * BLOCK] + bias[i, 2 * p + e]
-                scores[:, p * wide + e * BLOCK : p * wide + (e + 1) * BLOCK] = se
-                top = jnp.maximum(top, se)
+            scores[buf, :, p * wide : (p + 1) * wide] = s
+            top = jnp.maximum(top, jnp.maximum(s[:, :BLOCK], s[:, BLOCK:]))
         top = jnp.max(top, axis=1, keepdims=True)
-        total = jnp.zeros((wide, BLOCK), F32)
         mixed = jnp.zeros((wide, BLOCK), F32)
         for p in range(listed // 2):
-            e = jnp.exp(scores[:, p * wide : (p + 1) * wide] - top)
-            total += e[:, :BLOCK] + e[:, BLOCK:]
-            mixed += jnp.dot(e.astype(BF16), kv_list[p * wide : (p + 1) * wide], preferred_element_type=F32)
-        mixed = mixed / jnp.sum(total, axis=1, keepdims=True)
+            e = jnp.exp(scores[buf, :, p * wide : (p + 1) * wide] - top).astype(BF16)
+            mixed += jnp.dot(e, kv_list[buf, 1, p * wide : (p + 1) * wide], preferred_element_type=F32)
+        mixed = mixed / pltpu.roll(mixed, HEAD, 1)
         both = jnp.where(low, pltpu.roll(mixed[:BLOCK], HEAD, 1), mixed[BLOCK:])
         attn[t] = jnp.where(i < live[0], both, 0.0).astype(BF16)
 
-    def step(u, _):
-        t = lax.rem(u + 1, chips)
-        attend(t)
-
-        @pl.when(u < chips - 1)
-        def _():
+    for n, t in enumerate((2, 1, 3, 0)):
+        attend(t, n % 2)
+        if t > 0:
             attn_copy(t).start()
-
-        return 0
-
-    lax.fori_loop(0, qblocks, step, 0)
 
     for d in far:
         attn_copy(d).wait_recv()
@@ -541,6 +530,7 @@
         any_space = pl.BlockSpec(memory_space=pl.ANY)
         smem = pl.BlockSpec(memory_space=pltpu.SMEM)
         scratch = [
+            pltpu.VMEM((rows_q, feats), BF16),
             pltpu.VMEM((shards, BLOCK, feats), BF16),
             pltpu.VMEM((chips, BLOCK, feats), BF16),
             pltpu.VMEM((far, BLOCK, feats), BF16),
@@ -550,14 +540,14 @@
             pltpu.VMEM(v_weight.shape, BF16),
             pltpu.VMEM((width, 2 * kv_cols), BF16),
             pltpu.VMEM(o_weight.shape, BF16),
-            pltpu.VMEM((rows_m // chips, feats), BF16),
+            pltpu.VMEM((rows_m, feats), BF16),
             pltpu.VMEM((CHUNKS, far, rows_j, feats), BF16),
             pltpu.VMEM((CHUNKS, chips, half, feats), BF16),
             pltpu.VMEM((CHUNKS, KV_HEADS, piece, BLOCK, 2 * HEAD), BF16),
             pltpu.VMEM((3 * pool_blocks, BLOCK, 2 * HEAD), BF16),
-            pltpu.VMEM((listed * BLOCK, 2 * HEAD), BF16),
+            pltpu.VMEM((2, 2, listed * BLOCK, 2 * HEAD), BF16),
             pltpu.VMEM((qblocks, 2 * BLOCK, 2 * HEAD), BF16),
-            pltpu.VMEM((2 * BLOCK, listed * BLOCK), F32),
+            pltpu.VMEM((2, 2 * BLOCK, listed * BLOCK), F32),
             pltpu.SMEM((qblocks, listed), F32),
             pltpu.VMEM((columns, far, width // columns, feats), BF16),
             pltpu.VMEM((chips, BLOCK, 2 * HEAD), BF16),
@@ -595,7 +585,7 @@
             out_specs=pl.BlockSpec(memory_space=pltpu.VMEM),
             scratch_shapes=scratch,
             compiler_params=pltpu.CompilerParams(
-                collective_id=0, has_side_effects=True, vmem_limit_bytes=60 << 20
+                collective_id=0, has_side_effects=True, vmem_limit_bytes=215 << 18
             ),
         )(queries, mold, q_weight, k_weight, v_weight, o_weight, lists, live)
 

time: 65.2 us -> 63.7 us (0.977)
  Pallas kernels: 62.8 us -> 61.6 us
    pallas_call x1, Pallas kernels: 62.8 us -> 61.6 us  [step(): pl.pallas_call(functools.partial(kernel, chips, regions), out_shape=jax.S...]
    unnamed x1 -> x3, local copies, waits for them, and re-layouts: 1.57 us -> 1.33 us
where the time goes in v3:
time: 63.7 us; the launch traced here: 63.6 us
  Pallas kernels  61.6 us (97%)
  local copies, waits for them, and re-layouts  1.33 us (2%)
  between operations  0.67 us (1%)
    pallas_call x1, Pallas kernels, step(): pl.pallas_call(functools.partial(kernel, chips, regions), out_shape=jax.S...  61.6 us
    unnamed x3, local copies, waits for them, and re-layouts  1.33 us

profile of v3, /device:TPU:1, one launch (start us, length us, event | category | flops | bytes accessed | tf_op | source)
XLA Modules:
  0.0 63.6 jit_solution(12688220058795236790)
XLA Ops:
  0.7 0.0 copy-start
  0.7 0.7 %copy-done = s32[4,16]{1,0:T(4,128)S(1)} copy-done((s32[4,16]{1,0:T(4,128)S(1)}, s32[4,16]{1,0:T(4,128)}, u32[]{:S(2)}) %copy-start) | copy-done | bytes 280
  1.3 61.6 %shard_map.82 = bf16[512,128]{1,0:T(8,128)(2,1)S(1)} custom-call(bf16[512,128]{1,0:T(8,128)(2,1)} %queries.1, bf16[2048,128]{1,0:T(8,128)(2,1)} %mold.1, bf16[1024,128]{1,0:T(8,128)(2,1)} %q_weight.1, bf16[1024,256]{1,0:T(8,128)(2,1)} %k_weight.1, bf16[1024,256]{1,0:T(8,128)(2,1)} %v_weight.1, bf16[128,1024]{1,0:T(8,128)(2,1)} %o_weight.1, ...), custom_call_target="tpu_custom_call" | custom-call | tf_op jit(solution)/shard_map/pallas_call | solution.py:581
  62.9 0.7 %copy.11 = bf16[512,128]{1,0:T(8,128)(2,1)} copy(bf16[512,128]{1,0:T(8,128)(2,1)S(1)} %shard_map.82) | data formatting | bytes 262144
Async XLA Ops:
  0.7 0.7 %copy-start = (s32[4,16]{1,0:T(4,128)S(1)}, s32[4,16]{1,0:T(4,128)}, u32[]{:S(2)}) copy-start(s32[4,16]{1,0:T(4,128)} %lists.1) | copy-start | bytes 772

commit v4 on v3

--- a/solution.py
+++ b/solution.py
@@ -219,7 +219,7 @@
         )
 
     for j in range(CHUNKS):
-        for d in far:
+        for d in (2, 1, 3):
             mold_z_copy(j, d).start()
 
     def mold_src(j, d, side):
@@ -305,6 +305,8 @@
 
     q_core(0).start()
     for d in far:
+        q_z_copy(d).start()
+    for d in far:
         w1_copy(d).wait_recv()
     for e in range(1, side_x):
         w2_copy(e, True).start()
@@ -316,13 +318,9 @@
         w2_copy(e, False).wait_recv()
     for e in range(1, side_y):
         w3_copy(e, True).start()
-    for e in range(1, side_y):
-        o2_copy(e, False).wait_recv()
-    for e in range(1, side_x):
-        o3_copy(e, True).start()
 
     for j in range(CHUNKS):
-        for d in far:
+        for d in (2, 1, 3):
             mold_z_copy(j, d).wait_recv()
             mold_c_copy(j, d).start()
         total = jnp.zeros((half, wkv.shape[1]), F32)
@@ -343,8 +341,10 @@
         kv_sib(j, 0).start()
         kv_core(0, j, 0).start()
         if j == 0:
-            for d in far:
-                q_z_copy(d).start()
+            for e in range(1, side_y):
+                o2_copy(e, False).wait_recv()
+            for e in range(1, side_x):
+                o3_copy(e, True).start()
 
     def forward(j):
         for t in range(3):

time: 63.7 us -> 63.2 us (level)
  no operation moved by 1% of the time
where the time goes in v4:
time: 63.2 us; the launch traced here: 63.1 us
  Pallas kernels  61.1 us (97%)
  local copies, waits for them, and re-layouts  1.33 us (2%)
  between operations  0.67 us (1%)
    pallas_call x1, Pallas kernels, step(): pl.pallas_call(functools.partial(kernel, chips, regions), out_shape=jax.S...  61.1 us
    unnamed x3, local copies, waits for them, and re-layouts  1.33 us

profile of v4, /device:TPU:1, one launch (start us, length us, event | category | flops | bytes accessed | tf_op | source)
XLA Modules:
  0.0 63.1 jit_solution(9892451075038582231)
XLA Ops:
  0.7 0.0 copy-start
  0.7 0.7 %copy-done = s32[4,16]{1,0:T(4,128)S(1)} copy-done((s32[4,16]{1,0:T(4,128)S(1)}, s32[4,16]{1,0:T(4,128)}, u32[]{:S(2)}) %copy-start) | copy-done | bytes 280
  1.3 61.1 %shard_map.82 = bf16[512,128]{1,0:T(8,128)(2,1)S(1)} custom-call(bf16[512,128]{1,0:T(8,128)(2,1)} %queries.1, bf16[2048,128]{1,0:T(8,128)(2,1)} %mold.1, bf16[1024,128]{1,0:T(8,128)(2,1)} %q_weight.1, bf16[1024,256]{1,0:T(8,128)(2,1)} %k_weight.1, bf16[1024,256]{1,0:T(8,128)(2,1)} %v_weight.1, bf16[128,1024]{1,0:T(8,128)(2,1)} %o_weight.1, ...), custom_call_target="tpu_custom_call" | custom-call | tf_op jit(solution)/shard_map/pallas_call | solution.py:581
  62.4 0.7 %copy.11 = bf16[512,128]{1,0:T(8,128)(2,1)} copy(bf16[512,128]{1,0:T(8,128)(2,1)S(1)} %shard_map.82) | data formatting | bytes 262144
Async XLA Ops:
  0.7 0.7 %copy-start = (s32[4,16]{1,0:T(4,128)S(1)}, s32[4,16]{1,0:T(4,128)}, u32[]{:S(2)}) copy-start(s32[4,16]{1,0:T(4,128)} %lists.1) | copy-start | bytes 772

commit v5 on v4

--- a/solution.py
+++ b/solution.py
@@ -355,11 +355,11 @@
                 kv_x(j, at).start()
             kv_core(slot, j, at).start()
 
-    forward(0)
-
     for d in far:
         q_z_got(d).wait_recv()
         q_core(d).start()
+    forward(0)
+
     for e in range(1, side_y):
         w3_copy(e, False).wait_recv()
     for d in near:

time: 63.2 us -> 63.1 us (level)
  no operation moved by 1% of the time
where the time goes in v5:
time: 63.1 us; the launch traced here: 63 us
  Pallas kernels  61 us (97%)
  local copies, waits for them, and re-layouts  1.33 us (2%)
  between operations  0.67 us (1%)
    pallas_call x1, Pallas kernels, step(): pl.pallas_call(functools.partial(kernel, chips, regions), out_shape=jax.S...  61 us
    unnamed x3, local copies, waits for them, and re-layouts  1.33 us

profile of v5, /device:TPU:1, one launch (start us, length us, event | category | flops | bytes accessed | tf_op | source)
XLA Modules:
  0.0 63.0 jit_solution(879959663753779702)
XLA Ops:
  0.7 0.0 copy-start
  0.7 0.7 %copy-done = s32[4,16]{1,0:T(4,128)S(1)} copy-done((s32[4,16]{1,0:T(4,128)S(1)}, s32[4,16]{1,0:T(4,128)}, u32[]{:S(2)}) %copy-start) | copy-done | bytes 280
  1.3 61.0 %shard_map.82 = bf16[512,128]{1,0:T(8,128)(2,1)S(1)} custom-call(bf16[512,128]{1,0:T(8,128)(2,1)} %queries.1, bf16[2048,128]{1,0:T(8,128)(2,1)} %mold.1, bf16[1024,128]{1,0:T(8,128)(2,1)} %q_weight.1, bf16[1024,256]{1,0:T(8,128)(2,1)} %k_weight.1, bf16[1024,256]{1,0:T(8,128)(2,1)} %v_weight.1, bf16[128,1024]{1,0:T(8,128)(2,1)} %o_weight.1, ...), custom_call_target="tpu_custom_call" | custom-call | tf_op jit(solution)/shard_map/pallas_call | solution.py:581
  62.3 0.7 %copy.11 = bf16[512,128]{1,0:T(8,128)(2,1)} copy(bf16[512,128]{1,0:T(8,128)(2,1)S(1)} %shard_map.82) | data formatting | bytes 262144
Async XLA Ops:
  0.7 0.7 %copy-start = (s32[4,16]{1,0:T(4,128)S(1)}, s32[4,16]{1,0:T(4,128)}, u32[]{:S(2)}) copy-start(s32[4,16]{1,0:T(4,128)} %lists.1) | copy-start | bytes 772

commit v6 on v5

--- a/solution.py
+++ b/solution.py
@@ -350,9 +350,9 @@
         for t in range(3):
             kv_z_got(j, t).wait_recv()
             slot, at = z_arrivals[t]
-            kv_sib(j, t + 1).start()
             if slot == 1:
                 kv_x(j, at).start()
+            kv_sib(j, t + 1).start()
             kv_core(slot, j, at).start()
 
     for d in far:

time: 63.1 us -> 63.1 us (level)
  no operation moved by 1% of the time
where the time goes in v6:
time: 63.1 us; the launch traced here: 62.9 us
  Pallas kernels  60.9 us (97%)
  local copies, waits for them, and re-layouts  1.33 us (2%)
  between operations  0.67 us (1%)
    pallas_call x1, Pallas kernels, step(): pl.pallas_call(functools.partial(kernel, chips, regions), out_shape=jax.S...  60.9 us
    unnamed x3, local copies, waits for them, and re-layouts  1.33 us

profile of v6, /device:TPU:1, one launch (start us, length us, event | category | flops | bytes accessed | tf_op | source)
XLA Modules:
  0.0 62.9 jit_solution(513169570263275175)
XLA Ops:
  0.7 0.0 copy-start
  0.7 0.7 %copy-done = s32[4,16]{1,0:T(4,128)S(1)} copy-done((s32[4,16]{1,0:T(4,128)S(1)}, s32[4,16]{1,0:T(4,128)}, u32[]{:S(2)}) %copy-start) | copy-done | bytes 280
  1.3 60.9 %shard_map.82 = bf16[512,128]{1,0:T(8,128)(2,1)S(1)} custom-call(bf16[512,128]{1,0:T(8,128)(2,1)} %queries.1, bf16[2048,128]{1,0:T(8,128)(2,1)} %mold.1, bf16[1024,128]{1,0:T(8,128)(2,1)} %q_weight.1, bf16[1024,256]{1,0:T(8,128)(2,1)} %k_weight.1, bf16[1024,256]{1,0:T(8,128)(2,1)} %v_weight.1, bf16[128,1024]{1,0:T(8,128)(2,1)} %o_weight.1, ...), custom_call_target="tpu_custom_call" | custom-call | tf_op jit(solution)/shard_map/pallas_call | solution.py:581
  62.3 0.7 %copy.11 = bf16[512,128]{1,0:T(8,128)(2,1)} copy(bf16[512,128]{1,0:T(8,128)(2,1)S(1)} %shard_map.82) | data formatting | bytes 262144
Async XLA Ops:
  0.7 0.7 %copy-start = (s32[4,16]{1,0:T(4,128)S(1)}, s32[4,16]{1,0:T(4,128)}, u32[]{:S(2)}) copy-start(s32[4,16]{1,0:T(4,128)} %lists.1) | copy-start | bytes 772
